TPU v7x, 32 devices: a whole 2x2x4 slice. The times are simulated.
32 devices in a mesh: seq: 16 (over z, y, x), tp: 2 (over core).
Axes of the slice: x: 2, y: 2, z: 4, core: 2. Of those that a mesh axis runs over, the one named last changes fastest.
Arguments:
- tokens: bfloat16 [1024, 2, 1024], P('seq'), may hold values from -6 to 6
- d_out: float32 [1024, 2, 1024], P('seq'), may hold values from -6 to 6
- norm1_gain: float32 [2, 1024], replicated, may hold values from 0.1 to 1.9
- norm1_shift: float32 [2, 1024], replicated, may hold values from -3 to 3
- w_qkv: bfloat16 [2, 1024, 3, 1024], P(None, None, None, 'tp'), may hold values from -0.1875 to 0.1875
- b_qkv: float32 [2, 3, 1024], P(None, None, 'tp'), may hold values from -3 to 3
- w_out: bfloat16 [2, 1024, 1024], P(None, 'tp'), may hold values from -1.5 to 1.5
- b_out: float32 [2, 1024], replicated, may hold values from -3 to 3
- norm2_gain: float32 [2, 1024], replicated, may hold values from 0.1 to 1.9
- norm2_shift: float32 [2, 1024], replicated, may hold values from -3 to 3
- w_up: bfloat16 [2, 1024, 4096], P(None, None, 'tp'), may hold values from -0.1875 to 0.1875
- b_up: float32 [2, 4096], P(None, 'tp'), may hold values from -3 to 3
- w_down: bfloat16 [2, 4096, 1024], P(None, 'tp'), may hold values from -0.09375 to 0.09375
- b_down: float32 [2, 1024], replicated, may hold values from -3 to 3
- episode_frames: int32 [2, 4], replicated, may hold values from 0 to 4, as said below
- live: int32 [1024, 2], P('seq'), may hold values from 0 to 1, as said below
Outputs:
- out: float32 [1024, 2, 1024], P('seq')
- d_x: float32 [1024, 2, 1024], P('seq')
- g_norm1_gain: float32 [2, 1024], P(None, 'seq')
- g_norm1_shift: float32 [2, 1024], P(None, 'seq')
- g_w_qkv: float32 [2, 1024, 3, 1024], P(None, 'seq', None, 'tp')
- g_b_qkv: float32 [2, 3, 1024], P(None, None, 'tp')
- g_w_out: float32 [2, 1024, 1024], P(None, 'tp', 'seq')
- g_b_out: float32 [2, 1024], P(None, 'seq')
- g_norm2_gain: float32 [2, 1024], P(None, 'seq')
- g_norm2_shift: float32 [2, 1024], P(None, 'seq')
- g_w_up: float32 [2, 1024, 4096], P(None, 'seq', 'tp')
- g_b_up: float32 [2, 4096], P(None, 'tp')
- g_w_down: float32 [2, 4096, 1024], P(None, 'tp', 'seq')
- g_b_down: float32 [2, 1024], P(None, 'seq')
Inputs may be any that keep to these rules, and one draw needn't show every extreme that they name: `episode_frames`: each row sums to 4. In every draw one lane, drawn from the seed, is a single episode of all 4 frames followed by empty slots; every other lane holds 4 episodes of one frame or more. Padding only at the end of an episode, at most half of 256 tokens of its last frame; the first token of every episode is live.
All inputs are finite; a program needn't handle non-finite values.
Results may differ from a plain program's by a relative error of at most 0.024.
Values may be sent and summed in bfloat16 or wider, within the bound.
A program may use at most 256 MiB of HBM per device.

v0:
```python
import math

import jax
import jax.numpy as jnp
import numpy as np
from jax import lax
from jax.experimental import pallas as pl
from jax.experimental.pallas import tpu as pltpu
from jax.sharding import PartitionSpec as P

HEAD_DIM = 64
GRID = 16
FRAME = 256
LAYERS = 2
MICRO = 2


EPSILON = 1e-06
MASKED = -1e30
SCORE_SCALE = 0.125


def layer_norm(stream, norm_gain, norm_shift):
    center = stream - jnp.mean(stream, axis=-1, keepdims=True)
    spread = jnp.mean(center * center, axis=-1, keepdims=True)
    return center * lax.rsqrt(spread + EPSILON) * norm_gain + norm_shift


def rotate(values, frame_place, row_place, column_place):
    frequency = jnp.exp(jnp.arange(10, dtype=jnp.float32) * (-math.log(10000.0) / 10.0))
    pieces = []
    for section, place in enumerate((frame_place, row_place, column_place)):
        lower = values[..., 20 * section : 20 * section + 10]
        upper = values[..., 20 * section + 10 : 20 * section + 20]
        angles = place.astype(jnp.float32)[..., None, None] * frequency
        cosine = jnp.cos(angles)
        sine_part = jnp.sin(angles)
        pieces.append(lower * cosine - upper * sine_part)
        pieces.append(lower * sine_part + upper * cosine)
    pieces.append(values[..., 60:])
    return jnp.concatenate(pieces, axis=-1)


def episode_tags(frame_counts, positions):
    endings = jnp.cumsum(frame_counts) * FRAME
    passed = (positions[:, None] >= endings[None, :]).astype(jnp.int32)
    episode = jnp.sum(passed, axis=1)
    opening = jnp.sum(passed * frame_counts[None, :], axis=1)
    frame_index = positions // FRAME - opening
    within = positions % FRAME
    return (episode, frame_index, within // GRID, within % GRID)


def gelu_exact(values):
    return jax.nn.gelu(values, approximate=False)


def sum_heads(partial_sum):
    return lax.psum(partial_sum.astype(jnp.bfloat16), "tp").astype(jnp.float32)


def sum_inputs(partial_sum):
    return lax.psum(partial_sum.astype(jnp.bfloat16), "tp").astype(jnp.float32)


def lane_scores(query, keys_all, lane_index, query_tags, key_tags):
    head_count = query.shape[2] // HEAD_DIM
    query_lane = lax.dynamic_index_in_dim(query, lane_index, 1, False).reshape(
        query.shape[0], head_count, HEAD_DIM
    )
    keys_lane = lax.dynamic_index_in_dim(keys_all, lane_index, 1, False).reshape(
        keys_all.shape[0], head_count, HEAD_DIM
    )
    query_episode, query_frame = [
        lax.dynamic_index_in_dim(item, lane_index, 1, False) for item in query_tags
    ]
    key_episode, key_frame, key_live = [
        lax.dynamic_index_in_dim(item, lane_index, 1, False) for item in key_tags
    ]
    allowed = (
        (query_episode[:, None] == key_episode[None, :])
        & (key_frame[None, :] <= query_frame[:, None])
        & (key_live[None, :] > 0)
    )
    scores = (
        jnp.einsum("qhd,khd->hqk", query_lane, keys_lane, preferred_element_type=jnp.float32)
        * SCORE_SCALE
    )
    return (jnp.where(allowed[None], scores, MASKED), query_lane, keys_lane)


def attend_forward(query, keys_all, values_all, query_tags, key_tags):
    rows_dev, lane_count, features = query.shape
    head_count = features // HEAD_DIM

    def one_lane(lane_index, carry):
        scores, query_lane, keys_lane = lane_scores(
            query, keys_all, lane_index, query_tags, key_tags
        )
        highest = jnp.max(scores, axis=-1, keepdims=True)
        shifted = jnp.exp(scores - highest)
        summed = jnp.sum(shifted, axis=-1, keepdims=True)
        attention = (shifted / summed).astype(jnp.bfloat16)
        values_lane = lax.dynamic_index_in_dim(values_all, lane_index, 1, False).reshape(
            values_all.shape[0], head_count, HEAD_DIM
        )
        result = jnp.einsum(
            "hqk,khd->qhd", attention, values_lane, preferred_element_type=jnp.float32
        ).reshape(rows_dev, 1, features)
        log_total = (highest + jnp.log(summed))[None, :, :, 0]
        return (result, log_total)

    initial = (
        jnp.zeros((rows_dev, lane_count, features), jnp.float32),
        jnp.zeros((lane_count, head_count, rows_dev), jnp.float32),
    )
    return lax.fori_loop(0, lane_count, one_lane, initial)


def attend_backward(query, keys_all, values_all, log_total, grad_mixed, query_tags, key_tags):
    rows_dev, lane_count, features = query.shape
    head_count = features // HEAD_DIM
    key_rows = keys_all.shape[0]

    def one_lane(lane_index, carry):
        scores, query_lane, keys_lane = lane_scores(
            query, keys_all, lane_index, query_tags, key_tags
        )
        values_lane = lax.dynamic_index_in_dim(values_all, lane_index, 1, False).reshape(
            key_rows, head_count, HEAD_DIM
        )
        grad_lane = lax.dynamic_index_in_dim(grad_mixed, lane_index, 1, False).reshape(
            rows_dev, head_count, HEAD_DIM
        )
        attention = jnp.exp(
            scores - lax.dynamic_index_in_dim(log_total, lane_index, 0, False)[:, :, None]
        )
        grad_attention = jnp.einsum(
            "qhd,khd->hqk", grad_lane, values_lane, preferred_element_type=jnp.float32
        )
        inner = jnp.sum(attention * grad_attention, axis=-1, keepdims=True)
        grad_scores = (attention * (grad_attention - inner)).astype(jnp.bfloat16)
        query_part = (
            jnp.einsum("hqk,khd->qhd", grad_scores, keys_lane, preferred_element_type=jnp.float32)
            * SCORE_SCALE
        )
        key_part = (
            jnp.einsum("hqk,qhd->khd", grad_scores, query_lane, preferred_element_type=jnp.float32)
            * SCORE_SCALE
        )
        value_part = jnp.einsum(
            "hqk,qhd->khd",
            attention.astype(jnp.bfloat16),
            grad_lane,
            preferred_element_type=jnp.float32,
        )
        stacked = jnp.stack(
            [key_part.reshape(key_rows, features), value_part.reshape(key_rows, features)], axis=1
        )
        key_terms = stacked[:, None]
        grad_query = query_part.reshape(rows_dev, 1, features)
        return (grad_query, key_terms)

    initial = (
        jnp.zeros((rows_dev, lane_count, features), jnp.float32),
        jnp.zeros((key_rows, lane_count, 2, features), jnp.float32),
    )
    return lax.fori_loop(0, lane_count, one_lane, initial)


def front(stream, layer_index, params, query_tags, key_tags, positions):
    (
        gain_one,
        shift_one,
        mat_qkv,
        bias_qkv,
        mat_out,
        bias_out,
        gain_two,
        shift_two,
        mat_up,
        bias_up,
        mat_down,
        bias_down,
    ) = [item[layer_index] for item in params]
    rows_dev, lane_count, width = stream.shape
    features = mat_qkv.shape[2]
    head_count = features // HEAD_DIM
    frame_place, row_place, column_place = positions
    first = layer_norm(stream, gain_one, shift_one).astype(jnp.bfloat16)
    projected = (
        jnp.einsum("tbd,dcf->tbcf", first, mat_qkv, preferred_element_type=jnp.float32) + bias_qkv
    )
    split = projected.reshape(rows_dev, lane_count, 3, head_count, HEAD_DIM)
    query = (
        rotate(split[:, :, 0], frame_place, row_place, column_place)
        .reshape(rows_dev, lane_count, features)
        .astype(jnp.bfloat16)
    )
    keys = (
        rotate(split[:, :, 1], frame_place, row_place, column_place)
        .reshape(rows_dev, lane_count, features)
        .astype(jnp.bfloat16)
    )
    values = projected[:, :, 2].astype(jnp.bfloat16)
    keys_all, values_all = (
        lax.all_gather(keys, "seq", axis=0, tiled=True),
        lax.all_gather(values, "seq", axis=0, tiled=True),
    )
    mixed_full, log_total = attend_forward(query, keys_all, values_all, query_tags, key_tags)
    mixed = mixed_full.astype(jnp.bfloat16)
    middle = (
        stream
        + sum_heads(jnp.einsum("tbf,fd->tbd", mixed, mat_out, preferred_element_type=jnp.float32))
        + bias_out
    )
    second = layer_norm(middle, gain_two, shift_two).astype(jnp.bfloat16)
    hidden = jnp.einsum("tbd,df->tbf", second, mat_up, preferred_element_type=jnp.float32) + bias_up
    activation = gelu_exact(hidden).astype(jnp.bfloat16)
    return (
        first,
        query,
        keys_all,
        values_all,
        log_total,
        mixed,
        middle,
        second,
        hidden,
        activation,
        mixed_full,
    )


def layer_backward(stream, gradient, layer_index, params, query_tags, key_tags, positions):
    (
        gain_one,
        shift_one,
        mat_qkv,
        bias_qkv,
        mat_out,
        bias_out,
        gain_two,
        shift_two,
        mat_up,
        bias_up,
        mat_down,
        bias_down,
    ) = [item[layer_index] for item in params]
    (
        first,
        query,
        keys_all,
        values_all,
        log_total,
        mixed,
        middle,
        second,
        hidden,
        activation,
        mixed_full,
    ) = front(stream, layer_index, params, query_tags, key_tags, positions)
    frame_place, row_place, column_place = positions
    rows_dev, lane_count, width = stream.shape
    features = query.shape[2]
    head_count = features // HEAD_DIM
    grad_low = gradient.astype(jnp.bfloat16)
    grad_w_down = jnp.einsum(
        "tbf,tbd->fd", activation, grad_low, preferred_element_type=jnp.float32
    )
    grad_b_down = jnp.sum(gradient, axis=(0, 1))
    grad_activation = jnp.einsum(
        "tbd,fd->tbf", grad_low, mat_down, preferred_element_type=jnp.float32
    )
    grad_hidden = jax.vjp(gelu_exact, hidden)[1](grad_activation)[0].astype(jnp.bfloat16)
    grad_b_up = jnp.sum(grad_hidden.astype(jnp.float32), axis=(0, 1))
    grad_w_up = jnp.einsum("tbd,tbf->df", second, grad_hidden, preferred_element_type=jnp.float32)
    grad_second = sum_inputs(
        jnp.einsum("tbf,df->tbd", grad_hidden, mat_up, preferred_element_type=jnp.float32)
    )
    middle_pull = jax.vjp(layer_norm, middle, gain_two, shift_two)[1]
    grad_inner, grad_gain_two, grad_shift_two = middle_pull(grad_second)
    grad_middle = gradient + grad_inner
    grad_b_out = jnp.sum(grad_middle, axis=(0, 1))
    middle_low = grad_middle.astype(jnp.bfloat16)
    grad_w_out = jnp.einsum("tbf,tbd->fd", mixed, middle_low, preferred_element_type=jnp.float32)
    grad_mixed = jnp.einsum(
        "tbd,fd->tbf", middle_low, mat_out, preferred_element_type=jnp.float32
    ).astype(jnp.bfloat16)
    grad_query, key_terms = attend_backward(
        query, keys_all, values_all, log_total, grad_mixed, query_tags, key_tags
    )
    returned = lax.psum_scatter(key_terms, "seq", scatter_dimension=0, tiled=True)
    turned_query = rotate(
        grad_query.reshape(rows_dev, lane_count, head_count, HEAD_DIM),
        -frame_place,
        -row_place,
        -column_place,
    )
    turned_keys = rotate(
        returned[:, :, 0].reshape(rows_dev, lane_count, head_count, HEAD_DIM),
        -frame_place,
        -row_place,
        -column_place,
    )
    grad_projected = jnp.stack(
        [
            turned_query.reshape(rows_dev, lane_count, features),
            turned_keys.reshape(rows_dev, lane_count, features),
            returned[:, :, 1],
        ],
        axis=2,
    ).astype(jnp.bfloat16)
    grad_b_qkv = jnp.sum(grad_projected.astype(jnp.float32), axis=(0, 1))
    grad_w_qkv = jnp.einsum(
        "tbd,tbcf->dcf", first, grad_projected, preferred_element_type=jnp.float32
    )
    grad_first = sum_inputs(
        jnp.einsum("tbcf,dcf->tbd", grad_projected, mat_qkv, preferred_element_type=jnp.float32)
    )
    first_pull = jax.vjp(layer_norm, stream, gain_one, shift_one)[1]
    grad_entry, grad_gain_one, grad_shift_one = first_pull(grad_first)
    grads = (
        grad_gain_one,
        grad_shift_one,
        grad_w_qkv,
        grad_b_qkv,
        grad_w_out,
        grad_b_out,
        grad_gain_two,
        grad_shift_two,
        grad_w_up,
        grad_b_up,
        grad_w_down,
        grad_b_down,
    )
    return (grad_middle + grad_entry, grads)


def per_device(
    tokens,
    d_out,
    norm1_gain,
    norm1_shift,
    w_qkv,
    b_qkv,
    w_out,
    b_out,
    norm2_gain,
    norm2_shift,
    w_up,
    b_up,
    w_down,
    b_down,
    episode_frames,
    live,
):
    rows_dev = tokens.shape[0]
    lane_count = tokens.shape[1] // MICRO
    total_rows = rows_dev * lax.axis_size("seq")
    local_positions = lax.axis_index("seq") * rows_dev + jnp.arange(rows_dev, dtype=jnp.int32)
    key_positions = jnp.arange(total_rows, dtype=jnp.int32)
    tagger = jax.vmap(episode_tags, in_axes=(0, None), out_axes=1)
    query_episode, query_frame, query_row, query_column = tagger(episode_frames, local_positions)
    key_episode, key_frame, key_row, key_column = tagger(episode_frames, key_positions)
    live_keys = lax.all_gather(live, "seq", axis=0, tiled=True)
    params = (
        norm1_gain,
        norm1_shift,
        w_qkv,
        b_qkv,
        w_out,
        b_out,
        norm2_gain,
        norm2_shift,
        w_up,
        b_up,
        w_down,
        b_down,
    )
    layer_grads = [None] * LAYERS
    outputs = []
    grad_tokens = []
    for micro_index in range(MICRO):
        first_lane = micro_index * lane_count
        last_lane = first_lane + lane_count
        query_tags = (query_episode[:, first_lane:last_lane], query_frame[:, first_lane:last_lane])
        key_tags = (
            key_episode[:, first_lane:last_lane],
            key_frame[:, first_lane:last_lane],
            live_keys[:, first_lane:last_lane],
        )
        positions = (
            query_frame[:, first_lane:last_lane],
            query_row[:, first_lane:last_lane],
            query_column[:, first_lane:last_lane],
        )
        stream = tokens[:, first_lane:last_lane].astype(jnp.float32)
        inputs = []
        gathered = []
        for layer_index in range(LAYERS):
            inputs.append(stream)
            layer_state = front(stream, layer_index, params, query_tags, key_tags, positions)
            gathered.append((layer_state[2], layer_state[3]))
            branch = jnp.einsum(
                "tbf,fd->tbd",
                layer_state[9],
                w_down[layer_index],
                preferred_element_type=jnp.float32,
            )
            stream = layer_state[6] + sum_heads(branch) + b_down[layer_index]
        outputs.append(stream)
        gradient = d_out[:, first_lane:last_lane]
        for layer_index in reversed(range(LAYERS)):
            gradient, grads = layer_backward(
                inputs[layer_index], gradient, layer_index, params, query_tags, key_tags, positions
            )
            if layer_grads[layer_index] is None:
                layer_grads[layer_index] = grads
            else:
                layer_grads[layer_index] = jax.tree.map(jnp.add, layer_grads[layer_index], grads)
        grad_tokens.append(gradient)
    stacked = [
        jnp.stack([layer_grads[layer_index][entry] for layer_index in range(LAYERS)])
        for entry in range(12)
    ]
    (
        grad_gain_one,
        grad_shift_one,
        grad_w_qkv,
        grad_b_qkv,
        grad_w_out,
        grad_b_out,
        grad_gain_two,
        grad_shift_two,
        grad_w_up,
        grad_b_up,
        grad_w_down,
        grad_b_down,
    ) = stacked
    in_sums = (
        lax.psum_scatter(grad_w_qkv, "seq", scatter_dimension=1, tiled=True),
        lax.psum_scatter(grad_w_up, "seq", scatter_dimension=1, tiled=True),
        lax.psum_scatter(grad_gain_one, "seq", scatter_dimension=1, tiled=True),
        lax.psum_scatter(grad_shift_one, "seq", scatter_dimension=1, tiled=True),
        lax.psum_scatter(grad_gain_two, "seq", scatter_dimension=1, tiled=True),
        lax.psum_scatter(grad_shift_two, "seq", scatter_dimension=1, tiled=True),
        lax.psum_scatter(grad_b_out, "seq", scatter_dimension=1, tiled=True),
        lax.psum_scatter(grad_b_down, "seq", scatter_dimension=1, tiled=True),
    )
    out_sums = (
        lax.psum_scatter(grad_w_out, "seq", scatter_dimension=2, tiled=True),
        lax.psum_scatter(grad_w_down, "seq", scatter_dimension=2, tiled=True),
    )
    bias_total = lax.psum((grad_b_qkv, grad_b_up), "seq")
    return (
        jnp.concatenate(outputs, axis=1),
        jnp.concatenate(grad_tokens, axis=1),
        in_sums[2],
        in_sums[3],
        in_sums[0],
        bias_total[0],
        out_sums[0],
        in_sums[6],
        in_sums[4],
        in_sums[5],
        in_sums[1],
        bias_total[1],
        out_sums[1],
        in_sums[7],
    )


MESH = pl.DeviceIdType.MESH
BF16 = jnp.bfloat16
F32 = jnp.float32
VMEM_BYTES = 60 * 1024 * 1024
PAIR = 128
VEC = 2048


def nn(left, right):
    return lax.dot_general(left, right, (((1,), (0,)), ((), ())), preferred_element_type=F32)


def nt(left, right):
    return lax.dot_general(left, right, (((1,), (1,)), ((), ())), preferred_element_type=F32)


def tn(left, right):
    return lax.dot_general(left, right, (((0,), (0,)), ((), ())), preferred_element_type=F32)


def at(start, size):
    return pl.ds(pl.multiple_of(start, size), size)


def repeat(count, body):
    def one(index, carry):
        body(index)
        return carry

    lax.fori_loop(0, count, one, 0)


def remote(src, dst, send, recv, seq, tp):
    return pltpu.make_async_remote_copy(
        src_ref=src,
        dst_ref=dst,
        send_sem=send,
        recv_sem=recv,
        device_id=(seq, tp),
        device_id_type=MESH,
    )


def hello(partners):
    barrier = pltpu.get_barrier_semaphore()
    for seq, tp in partners:
        pl.semaphore_signal(barrier, inc=1, device_id=(seq, tp), device_id_type=MESH)


def met(partners):
    pl.semaphore_wait(pltpu.get_barrier_semaphore(), len(partners))


def whole(array):
    zeros = (0,) * array.ndim
    return pl.BlockSpec(array.shape, lambda s: zeros, pipeline_mode=pl.Buffered(1))


def whole_out(shape):
    zeros = (0,) * len(shape)
    return pl.BlockSpec(shape, lambda s: zeros)


ANYWHERE = pl.BlockSpec(memory_space=pl.ANY)


def turn_row(table, place, section):
    frequency = np.exp(np.arange(10, dtype=np.float32) * np.float32(-math.log(10000.0) / 10.0))
    angle = place.astype(np.float32)[:, None] * frequency
    for base in range(20 * section, PAIR, HEAD_DIM):
        table[0, :, base : base + 10] = np.cos(angle)
        table[0, :, base + 10 : base + 20] = np.cos(angle)
        table[1, :, base : base + 10] = -np.sin(angle)
        table[2, :, base + 10 : base + 20] = np.sin(angle)


def turn_constants(frames):
    within, ahead = np.zeros((3, FRAME, PAIR), np.float32), np.zeros((3, frames, PAIR), np.float32)
    turn_row(within, np.arange(FRAME) // GRID, 1)
    turn_row(within, np.arange(FRAME) % GRID, 2)
    for base in range(60, PAIR, HEAD_DIM):
        within[0, :, base : base + 4] = 1.0
    turn_row(ahead, np.arange(frames), 0)
    return jnp.asarray(within), jnp.asarray(ahead)


def turn(values, tables, back=False):
    cosine, lower, upper = tables
    pieces = []
    for start in range(0, values.shape[1], PAIR):
        slab = values[:, start : start + PAIR]
        moved = pltpu.roll(slab, PAIR - 10, 1) * lower + pltpu.roll(slab, 10, 1) * upper
        pieces.append(slab * cosine - moved if back else slab * cosine + moved)
    return jnp.concatenate(pieces, axis=1)


def tables_of(fixed_ref, frames_ref, chunk):
    return [fixed_ref[i] + frames_ref[i, pl.ds(chunk, 1), :] for i in range(3)]


def normed(stream):
    center = stream - jnp.mean(stream, axis=-1, keepdims=True)
    spread = jnp.mean(center * center, axis=-1, keepdims=True)
    scale = lax.rsqrt(spread + EPSILON)
    return center * scale, scale


def norm_pull(grad, gain, unit, scale):
    scaled = grad * gain
    return scale * (
        scaled
        - jnp.mean(scaled, axis=-1, keepdims=True)
        - unit * jnp.mean(scaled * unit, axis=-1, keepdims=True)
    )


def keep_norm(unit, scale, unit_ref, scale_ref):
    unit_ref[...] = unit.astype(BF16)
    scale_ref[...] = jnp.broadcast_to(scale, scale_ref.shape)


def kept_norm(unit_ref, scale_ref):
    copies = unit_ref.shape[1] // scale_ref.shape[1]
    return unit_ref[...].astype(F32), jnp.concatenate([scale_ref[...]] * copies, axis=1)


def column_sum(values):
    return jnp.sum(values, axis=0, keepdims=True)


def gelu_both(hidden):
    normal = 0.5 + 0.5 * lax.erf(hidden * math.sqrt(0.5))
    density = jnp.exp(hidden * hidden * -0.5) * (1.0 / math.sqrt(2.0 * math.pi))
    return hidden * normal, normal + hidden * density


def project(stream, chunk, layer, pair, refs, outs, first_full):
    gain, shift, weight, bias, fixed, frames = refs
    qkv_ref, first_ref, unit_ref, scale_ref = outs
    unit, scale = normed(stream)
    keep_norm(unit, scale, unit_ref, scale_ref)
    first_full[...] = (unit * gain[layer : layer + 1, :] + shift[layer : layer + 1, :]).astype(BF16)
    first_ref[...] = first_full[:, at(pair * PAIR, PAIR)]
    cosine, lower, upper = tables_of(fixed, frames, chunk)

    def one(part):
        still = part == 2
        tables = (
            jnp.where(still, 1.0, cosine),
            jnp.where(still, 0.0, lower),
            jnp.where(still, 0.0, upper),
        )
        values = nn(first_full[...], weight[part]) + bias[part, layer : layer + 1, :]
        qkv_ref[part] = (turn(values, tables) * jnp.where(part == 0, SCORE_SCALE, 1.0)).astype(BF16)

    repeat(3, one)


class Relay:
    sems = 6

    def __init__(self, n, rows, buffer, other, sems, lives=None, live_other=None):
        self.n, self.rows, self.buffer, self.other = n, rows, buffer, other
        self.lives, self.live_other = lives, live_other
        self.z_send, self.z_recv, self.y_send, self.y_recv, self.c_send, self.c_recv = sems
        self.planes = n // 4
        self.me, self.core = lax.axis_index("seq"), lax.axis_index("tp")
        me = self.me
        self.x, self.y, self.z = lax.rem(me, 2), lax.rem(me // 2, 2), me // 4
        self.across = me + 2 - 4 * self.y

    @staticmethod
    def scratch(n):
        dma, planes = pltpu.SemaphoreType.DMA, n // 4
        shapes = [(planes, 2, 2)] * 2 + [(planes, 2)] * 2 + [(2 * planes,)] * 2
        return [dma(shape) for shape in shapes]

    @property
    def events(self):
        return self.planes

    def plane(self, step):
        return lax.rem(self.z + step, self.planes)

    def place(self, plane, lane):
        return plane * 4 + self.y * 2 + lane

    def reached(self):
        return [(step, far) for step in range(self.planes) for far in (0, 1) if step or far]

    def hello(self):
        barrier = pltpu.get_barrier_semaphore()
        partners = [(self.across, self.core), (self.me, 1 - self.core)]
        for step, far in self.reached():
            lane = 1 - self.x if far else self.x
            partners.append((self.place(self.plane(step), lane), self.core))
        for seq, tp in partners:
            pl.semaphore_signal(barrier, inc=1, device_id=(seq, tp), device_id_type=MESH)

    def met(self):
        pl.semaphore_wait(pltpu.get_barrier_semaphore(), 2 + len(self.reached()))

    def rows_of(self, side, seq):
        return self.buffer.at[side, at(seq * self.rows, self.rows), :]

    def block(self, side, pair):
        return self.buffer.at[side, at(pair * 2 * self.rows, 2 * self.rows), :]

    def items(self, pair):
        found = [self.block(self.core, pair)]
        if self.lives is not None:
            found.append(self.lives.at[at(pair * 2, 2)])
        return found

    def each(self, copy, what):
        for index in range(1 if self.lives is None else 2):
            getattr(copy(index), what)()

    def z_copy(self, step, far):
        def copy(index):
            lane = 1 - self.x if far else self.x
            if index == 0:
                source = self.other.at[self.core] if far else self.rows_of(self.core, self.me)
                target = self.rows_of(self.core, self.me)
            else:
                source = self.live_other if far else self.lives.at[self.me]
                target = self.lives.at[self.me]
            return remote(
                source,
                target,
                self.z_send.at[step, far, index],
                self.z_recv.at[step, far, index],
                self.place(self.plane(step), lane),
                self.core,
            )

        return copy

    def y_copy(self, plane, row):
        def copy(index):
            item = self.items(plane * 2 + row)[index]
            return remote(
                item,
                item,
                self.y_send.at[plane, index],
                self.y_recv.at[plane, index],
                self.across,
                self.core,
            )

        return copy

    def c_copy(self, pair, side):
        item = self.block(side, pair)
        return remote(
            item, item, self.c_send.at[pair], self.c_recv.at[pair], self.me, 1 - self.core
        )

    def begin(self):
        for step, far in self.reached():
            self.each(self.z_copy(step, far), "start")

    def arrive(self, event):
        for far in (0, 1) if event else (1,):
            self.each(self.z_copy(event, far), "wait_recv")
        plane = self.plane(self.planes - event)
        self.each(self.y_copy(plane, self.y), "start")
        self.c_copy(plane * 2 + self.y, self.core).start()

    def complete(self, event):
        plane = self.plane(self.planes - event)
        self.each(self.y_copy(plane, 1 - self.y), "wait_recv")
        self.c_copy(plane * 2 + 1 - self.y, self.core).start()

    def ready(self, event):
        plane = self.plane(self.planes - event)
        self.c_copy(plane * 2, 1 - self.core).wait_recv()
        self.c_copy(plane * 2 + 1, 1 - self.core).wait_recv()
        return plane

    def finish(self):
        for step, far in self.reached():
            self.each(self.z_copy(step, far), "wait_send")
        for plane in range(self.planes):
            self.each(self.y_copy(plane, self.y), "wait_send")
        for pair in range(2 * self.planes):
            self.c_copy(pair, self.core).wait_send()


def split_lanes(values, x, buffer, other, start, rows):
    half = values.shape[2] // 2
    zero, one = values[:, 0, :], values[:, 1, :]
    own, far = jnp.where(x == 0, zero, one), jnp.where(x == 0, one, zero)
    core = lax.axis_index("tp")
    own = jnp.where(core == 0, own[:, :half], own[:, half:]).astype(BF16)
    buffer[core, at(start, rows), :] = own
    for side in range(2):
        other[side] = far[:, side * half : (side + 1) * half].astype(BF16)


def gather_and_project(tokens, live, episode_frames, gain, shift, qkv, bias, fixed, ahead, n):
    rows, lanes, width = tokens.shape
    half = width // 2
    total = n * rows
    chunks = total // FRAME
    per_frame = FRAME // rows
    features = qkv.shape[3]
    slots = episode_frames.shape[1]

    def kernel(*refs):
        refs = list(refs)

        def take(count):
            taken = refs[:count]
            del refs[:count]
            return taken

        tokens_ref, live_ref, counts_ref, gain_ref, shift_ref, w_any, bias_ref = take(7)
        fixed_ref, ahead_ref = take(2)
        all_ref, mask_ref, frames_ref = take(3)
        qkv_ref, *projected = take(4)
        other, lives, live_other, weight, full, w_sem = take(6)
        relay = Relay(n, rows, all_ref, other, take(Relay.sems), lives, live_other)
        load = pltpu.make_async_copy(w_any.at[0], weight, w_sem)
        load.start()
        relay.hello()
        x, me = relay.x, relay.me
        split_lanes(tokens_ref[...].astype(F32), x, all_ref, other, me * rows, rows)
        lane = lax.broadcasted_iota(jnp.int32, (1, FRAME), 1)
        here = lane // rows == lax.rem(me, per_frame)
        tiles = []
        for index in range(lanes):
            alive = live_ref[index : index + 1, :].astype(F32)
            alive = jnp.where(here, jnp.concatenate([alive] * per_frame, axis=1), 0.0)
            tiles.append(jnp.broadcast_to(alive, (8, FRAME)))
        lives[me] = jnp.where(x == 0, tiles[0], tiles[1])
        live_other[...] = jnp.where(x == 0, tiles[1], tiles[0])
        relay.met()
        relay.begin()

        counts = [counts_ref[x, slot] for slot in range(slots)]
        episodes, openings = [], []
        for frame in range(chunks):
            end, episode, opening = 0, 0, 0
            for slot in range(slots):
                end = end + counts[slot]
                passed = frame >= end
                episode = episode + passed.astype(jnp.int32)
                opening = opening + jnp.where(passed, counts[slot], 0)
            episodes.append(episode)
            openings.append(frame - opening)
        for index in range(3):
            table = []
            for frame in range(chunks):
                line = jnp.zeros((1, PAIR), F32)
                for choice in range(chunks):
                    line = jnp.where(
                        openings[frame] == choice, ahead_ref[index, choice : choice + 1, :], line
                    )
                table.append(line)
            frames_ref[index] = jnp.concatenate(
                table + [jnp.zeros((8 - chunks, PAIR), F32)], axis=0
            )
        load.wait()

        def project_frame(frame):
            place = at(frame * FRAME, FRAME)
            stream = jnp.concatenate([all_ref[0, place, :], all_ref[1, place, :]], axis=1)
            project(
                stream.astype(F32),
                frame,
                0,
                me // 2,
                (gain_ref, shift_ref, weight, bias_ref, fixed_ref, frames_ref),
                [qkv_ref.at[:, place, :]] + [ref.at[place, :] for ref in projected],
                full,
            )

        for event in range(relay.events):
            relay.arrive(event)
            if event:
                relay.complete(event - 1)
            if event > 1:
                project_frame(relay.ready(event - 2))
        relay.complete(relay.events - 1)
        for event in range(max(0, relay.events - 2), relay.events):
            project_frame(relay.ready(event))
        relay.finish()

        for key_frame in range(chunks):
            alive = lives[key_frame * per_frame, 0:1, :]
            for part in range(1, per_frame):
                alive = alive + lives[key_frame * per_frame + part, 0:1, :]
            closed = (alive - 1.0) * -MASKED
            lines = []
            for query_frame in range(chunks):
                allowed = (episodes[query_frame] == episodes[key_frame]) & (
                    openings[key_frame] <= openings[query_frame]
                )
                lines.append(jnp.where(allowed, closed, MASKED))
            lines.append(jnp.zeros((PAIR - chunks, FRAME), F32))
            mask_ref[key_frame * FRAME : (key_frame + 1) * FRAME, :] = jnp.concatenate(
                lines, axis=0
            ).T.astype(BF16)

    in_vmem = pl.BlockSpec(memory_space=pltpu.VMEM)
    in_smem = pl.BlockSpec(memory_space=pltpu.SMEM)
    return pl.pallas_call(
        kernel,
        out_shape=(
            jax.ShapeDtypeStruct((2, total, half), BF16),
            jax.ShapeDtypeStruct((total, PAIR), BF16),
            jax.ShapeDtypeStruct((3, 8, PAIR), F32),
            jax.ShapeDtypeStruct((3, total, features), BF16),
            jax.ShapeDtypeStruct((total, PAIR), BF16),
            jax.ShapeDtypeStruct((total, width), BF16),
            jax.ShapeDtypeStruct((total, PAIR), F32),
        ),
        in_specs=[in_vmem, in_vmem, in_smem, in_vmem, in_vmem, ANYWHERE] + [in_vmem] * 3,
        out_specs=(in_vmem,) * 7,
        scratch_shapes=[
            pltpu.VMEM((2, rows, half), BF16),
            pltpu.VMEM((n, 8, FRAME), F32),
            pltpu.VMEM((8, FRAME), F32),
            pltpu.VMEM(qkv.shape[1:], BF16),
            pltpu.VMEM((FRAME, width), BF16),
            pltpu.SemaphoreType.DMA,
        ]
        + Relay.scratch(n),
        compiler_params=pltpu.CompilerParams(
            collective_id=0, has_side_effects=True, vmem_limit_bytes=VMEM_BYTES
        ),
        name="gather_and_project",
    )(tokens, live, episode_frames, gain, shift, qkv, bias, fixed, ahead)


def halves(ref):
    return jnp.concatenate([ref[0], ref[1]], axis=1).astype(F32)


def halves_spec(shape, chunks, behind, span=FRAME):
    return pl.BlockSpec(
        (2, span, shape[2]), lambda s: (0, jnp.clip(s - behind, 0, chunks - 1), 0)
    )


def layer_forward(layer, turned, key_bias, stream, mats, rows_of, next_refs, d_out, n, identity):
    _, total, features = turned.shape
    split = stream.ndim == 3
    width = mats[1].shape[1]
    rows_here = total // n
    hidden_units = mats[1].shape[2]
    chunks = total // FRAME
    heads = features // HEAD_DIM
    slabs = features // PAIR
    columns = 256
    last = next_refs is None
    b_out, gain, shift, b_up, b_down = rows_of
    mat_out, mat_up, mat_down = mats

    def kernel(*refs):
        refs = list(refs)

        def take(count):
            taken = refs[:count]
            del refs[:count]
            return taken

        q_ref, k_ref, v_ref, kb_ref, x_ref = take(5)
        wo_any, wu_any, wd_any = take(3)
        bo_ref, gain_ref, shift_ref, bu_ref, bd_ref = take(5)
        if not last:
            wq_any, ngain, nshift, nbias, fixed, frames = take(6)
        if d_out is not None:
            (d_ref,) = take(1)
        p_ref, r_ref, mixed_ref, unit_ref, scale_ref, second_ref, act_ref, gp_ref, x_out = take(9)
        if not last:
            next_outs = take(4)
        if d_out is not None:
            (d_all,) = take(1)
        wo, wu, wd, mid, full, next_full = take(6)
        if not last:
            (wq,) = take(1)
        a_send, a_recv, b_send, b_recv, w_sem, send_sem, recv_sem = take(7)
        relay = None
        if d_out is not None:
            buffer, other, d_sem = take(3)
            relay = Relay(n, rows_here, buffer, other, take(Relay.sems))

        step = pl.program_id(0)
        me, core = lax.axis_index("seq"), lax.axis_index("tp")

        items = [(wo_any, wo), (wu_any, wu), (wd_any, wd)]
        if not last:
            items.append((wq_any, wq))

        def load(index):
            source, target = items[index]
            return pltpu.make_async_copy(
                source.at[layer if index < 3 else layer + 1], target, w_sem.at[index]
            )

        def exchange(kind, chunk):
            source, target = ((a_send, a_recv), (b_send, b_recv))[kind]
            return remote(
                source.at[chunk],
                target.at[chunk],
                send_sem.at[kind, chunk],
                recv_sem.at[kind, chunk],
                me,
                1 - core,
            )

        @pl.when(step == 0)
        def _():
            for index in range(len(items)):
                load(index).start()
            if relay is None:
                hello([(me, 1 - core)])
            else:
                relay.hello()
                split_lanes(d_ref[...], relay.x, buffer, other, me * rows_here, rows_here)

        lane = lax.broadcasted_iota(jnp.int32, (1, PAIR), 1)
        sides = [(lane < HEAD_DIM).astype(F32).astype(BF16), (lane >= HEAD_DIM).astype(F32).astype(BF16)]
        for frame in range(chunks):

            @pl.when(step == frame)
            def _():
                keys = FRAME * (frame + 1)
                mask = kb_ref[:keys, :]
                asked = jnp.broadcast_to((lane == frame).astype(F32), (FRAME, PAIR)).astype(BF16)

                def two_slabs(couple):
                    def lanes_of(head):
                        return at((couple * 2 + head // 2) * PAIR, PAIR)

                    def score(head):
                        key = jnp.concatenate([k_ref[0, :keys, lanes_of(head)], mask], axis=1)
                        ask = q_ref[0, :, lanes_of(head)] * sides[head % 2]
                        return nt(jnp.concatenate([ask, asked], axis=1), key)

                    scores, sums = score(0), []
                    for head in range(4):
                        lanes, side = lanes_of(head), head % 2
                        following = score(head + 1) if head < 3 else None
                        highest = jnp.max(scores, axis=1, keepdims=True)
                        shifted = jnp.exp(scores - highest).astype(BF16)
                        p_ref[0, couple * 4 + head, :keys, :] = shifted.T
                        sums.append(nn(shifted, v_ref[0, :keys, lanes] * sides[side] + sides[1 - side]))
                        scores = following
                        if side == 1:
                            one, two = sums[head - 1 :]
                            low_side = lane < HEAD_DIM
                            divisor = 1.0 / jnp.where(
                                low_side, pltpu.roll(one, HEAD_DIM, 1), pltpu.roll(two, HEAD_DIM, 1)
                            )
                            r_ref[:, lanes] = divisor
                            mixed_ref[:, lanes] = (jnp.where(low_side, one, two) * divisor).astype(BF16)

                repeat(slabs // 2, two_slabs)

        @pl.when(step == 0)
        def _():
            load(0).wait()
            if relay is None:
                met([(me, 1 - core)])
            else:
                relay.met()
                relay.begin()

        @pl.when(step < chunks)
        def _():
            a_send[step] = nn(mixed_ref[...], wo[...]).astype(BF16)
            exchange(0, step).start()

        if relay is not None:
            for event in range(relay.events):

                @pl.when(step == 2 + event // 2)
                def _():
                    relay.arrive(event)

                @pl.when(step == 3 + event // 2)
                def _():
                    relay.complete(event)

            @pl.when(step == chunks + 1)
            def _():
                for event in range(relay.events):
                    relay.ready(event)
                relay.finish()
                pltpu.make_async_copy(buffer, d_all, d_sem).start()

        def feed_forward():
            chunk = step - 1
            middle = (halves(x_ref) if split else x_ref[...]) + (
                a_send[chunk].astype(F32) + a_recv[chunk].astype(F32)
            )
            middle = middle + bo_ref[layer : layer + 1, :]
            mid[lax.rem(chunk, 2)] = middle
            unit, scale = normed(middle)
            keep_norm(unit, scale, unit_ref, scale_ref)
            second = (unit * gain_ref[layer : layer + 1, :] + shift_ref[layer : layer + 1, :]).astype(BF16)
            full[...] = second
            second_ref[...] = full[:, at((me // 2) * PAIR, PAIR)]
            parts = [slice(start, start + columns) for start in range(0, hidden_units, columns)]
            hidden = nn(second, wu[:, parts[0]])
            for index, part in enumerate(parts):
                following = nn(second, wu[:, parts[index + 1]]) if index + 1 < len(parts) else None
                act, slope = gelu_both(hidden + bu_ref[layer : layer + 1, part])
                act_ref[:, part] = act.astype(BF16)
                gp_ref[:, part] = slope.astype(BF16)
                hidden = following
            b_send[chunk] = nn(act_ref[...], wd[...]).astype(BF16)

        def close():
            chunk = step - 2
            result = mid[lax.rem(chunk, 2)] + (b_send[chunk].astype(F32) + b_recv[chunk].astype(F32))
            result = result + bd_ref[layer : layer + 1, :]
            x_out[...] = result
            if not last:
                project(
                    result,
                    chunk,
                    layer + 1,
                    me // 2,
                    (ngain, nshift, wq, nbias, fixed, frames),
                    next_outs,
                    next_full,
                )

        @pl.when(step == 1)
        def _():
            load(1).wait()
            load(2).wait()

        @pl.when((step >= 1) & (step <= chunks))
        def _():
            exchange(0, step - 1).wait_recv()
            feed_forward()
            exchange(1, step - 1).start()

        if not last:

            @pl.when(step == 2)
            def _():
                load(3).wait()

        @pl.when(step >= 2)
        def _():
            exchange(1, step - 2).wait_recv()
            close()

        @pl.when(step == chunks + 1)
        def _():
            for kind in range(2):
                for chunk in range(chunks):
                    exchange(kind, chunk).wait_send()
            if relay is not None:
                pltpu.make_async_copy(buffer, d_all, d_sem).wait()

    def rows(columns, behind):
        return pl.BlockSpec(
            (FRAME, columns), lambda s: (jnp.clip(s - behind, 0, chunks - 1), 0)
        )

    def part_of(part):
        return pl.BlockSpec(
            (1, total, features), lambda s: (part, 0, 0), pipeline_mode=pl.Buffered(1)
        )

    in_specs = [
        pl.BlockSpec((1, FRAME, features), lambda s: (0, jnp.minimum(s, chunks - 1), 0)),
        part_of(1),
        part_of(2),
        whole(key_bias),
    ]
    in_specs += [halves_spec(stream.shape, chunks, 1) if split else rows(width, 1)]
    in_specs += [ANYWHERE] * 3 + [whole(item) for item in rows_of]
    operands = [turned, turned, turned, key_bias, stream, *mats, *rows_of]
    if not last:
        in_specs += [ANYWHERE] + [whole(item) for item in next_refs[1:]]
        operands += list(next_refs)
    if d_out is not None:
        in_specs += [whole(d_out)]
        operands += [d_out]
    out_shape = [
        jax.ShapeDtypeStruct((chunks, heads, total, FRAME), BF16),
        jax.ShapeDtypeStruct((total, features), F32),
        jax.ShapeDtypeStruct((total, features), BF16),
        jax.ShapeDtypeStruct((total, width), BF16),
        jax.ShapeDtypeStruct((total, PAIR), F32),
        jax.ShapeDtypeStruct((total, PAIR), BF16),
        jax.ShapeDtypeStruct((total, hidden_units), BF16),
        jax.ShapeDtypeStruct((total, hidden_units), BF16),
        jax.ShapeDtypeStruct((total, width), F32),
    ]
    out_specs = [
        pl.BlockSpec((1, heads, total, FRAME), lambda s: (jnp.minimum(s, chunks - 1), 0, 0, 0)),
        rows(features, 0),
        rows(features, 0),
        rows(width, 1),
        rows(PAIR, 1),
        rows(PAIR, 1),
        rows(hidden_units, 1),
        rows(hidden_units, 1),
        rows(width, 2),
    ]
    scratch = [
        pltpu.VMEM(mat_out.shape[1:], BF16),
        pltpu.VMEM(mat_up.shape[1:], BF16),
        pltpu.VMEM(mat_down.shape[1:], BF16),
        pltpu.VMEM((2, FRAME, width), F32),
        pltpu.VMEM((FRAME, width), BF16),
        pltpu.VMEM((FRAME, width), BF16),
    ]
    if not last:
        out_shape += [jax.ShapeDtypeStruct((3, total, features), BF16)]
        out_shape += [jax.ShapeDtypeStruct((total, PAIR), BF16)]
        out_shape += [jax.ShapeDtypeStruct((total, width), BF16)]
        out_shape += [jax.ShapeDtypeStruct((total, PAIR), F32)]
        out_specs += [
            pl.BlockSpec((3, FRAME, features), lambda s: (0, jnp.clip(s - 2, 0, chunks - 1), 0))
        ]
        out_specs += [rows(PAIR, 2), rows(width, 2), rows(PAIR, 2)]
    if d_out is not None:
        out_shape += [jax.ShapeDtypeStruct((2, total, width // 2), BF16)]
        out_specs += [ANYWHERE]
        scratch += [pltpu.VMEM(next_refs[0].shape[1:], BF16)]
    scratch += [pltpu.VMEM((chunks, FRAME, width), BF16)] * 4
    scratch += [
        pltpu.SemaphoreType.DMA((4,)),
        pltpu.SemaphoreType.DMA((2, chunks)),
        pltpu.SemaphoreType.DMA((2, chunks)),
    ]
    if d_out is not None:
        scratch += [
            pltpu.VMEM((2, total, width // 2), BF16),
            pltpu.VMEM((2, rows_here, width // 2), BF16),
            pltpu.SemaphoreType.DMA,
        ]
        scratch += Relay.scratch(n)
    return pl.pallas_call(
        kernel,
        grid=(chunks + 2,),
        out_shape=out_shape,
        in_specs=in_specs,
        out_specs=out_specs,
        scratch_shapes=scratch,
        compiler_params=pltpu.CompilerParams(
            collective_id=identity, has_side_effects=True, vmem_limit_bytes=VMEM_BYTES
        ),
        name=f"layer_forward_{layer}",
    )(*operands)


class Swap:
    def __init__(self, ships, lane_rows):
        self.ships, self.lane_rows = ships, lane_rows
        self.count = len(ships) + len(lane_rows)

    def operands(self):
        return [*self.ships, *[item for item, _ in self.lane_rows]]

    def in_specs(self):
        return [whole(item) for item in self.ships] + [ANYWHERE] * len(self.lane_rows)

    def outputs(self):
        shapes, specs = [], []
        for item in self.ships:
            shape = (item.shape[0] // 2, item.shape[1])
            shapes.append(jax.ShapeDtypeStruct(shape, F32))
            specs.append(whole_out(shape))
        for item, count in self.lane_rows:
            shapes.append(jax.ShapeDtypeStruct((count or item.shape[0], item.shape[1]), item.dtype))
            specs.append(ANYWHERE)
        return shapes, specs

    def scratch(self):
        if not self.count:
            return []
        buffers = [pltpu.VMEM((item.shape[0] // 2, item.shape[1]), BF16) for item in self.ships]
        return buffers * 2 + [pltpu.SemaphoreType.DMA((self.count,))] * 2

    def bind(self, sources, targets, scratch):
        ships = len(self.ships)
        me, core = lax.axis_index("seq"), lax.axis_index("tp")
        x = lax.rem(me, 2)
        beside = me + 1 - 2 * x
        half = PAIR // 2

        def copy(index):
            if index < ships:
                source, target = scratch[index], scratch[ships + index]
            else:
                source, target = sources[index], targets[index]
                count = self.lane_rows[index - ships][1]
                if count:
                    source = source.at[at(beside * count, count), :]
            send, recv = scratch[2 * ships].at[index], scratch[2 * ships + 1].at[index]
            return remote(source, target, send, recv, beside, core)

        def start():
            for index in range(self.count):
                if index < ships:
                    scratch[index][...] = sources[index][at((1 - x) * half, half), :].astype(BF16)
                copy(index).start()

        def finish():
            for index in range(self.count):
                copy(index).wait_recv()
                if index < ships:
                    own = sources[index][at(x * half, half), :]
                    targets[index][...] = own + scratch[ships + index][...].astype(F32)
            for index in range(self.count):
                copy(index).wait_send()

        return start, finish


def attention_backward(
    probs, divisor, mixed, turned_qkv, grad_mixed, first, fixed, frames, swap, swap_qkv, identity
):
    _, total, features = turned_qkv.shape
    chunks = total // FRAME
    slabs = features // PAIR
    half = PAIR // 2

    def kernel(*refs):
        refs = list(refs)

        def take(count):
            taken = refs[:count]
            del refs[:count]
            return taken

        p_ref, r_ref, o_ref, q_ref, k_ref, v_ref, g_ref, first_ref, fixed_ref, frames_ref = take(10)
        sources = take(swap.count)
        dq_ref, dk_ref, dv_ref, qkv_out = take(4)
        targets = take(swap.count)
        dk_sum, dv_sum, first_turned = take(3)
        if swap_qkv:
            qkv_own, qkv_send, qkv_recv, qkv_sems = take(4)
        start, finish = swap.bind(sources, targets, refs)

        step = pl.program_id(0)
        me, core = lax.axis_index("seq"), lax.axis_index("tp")
        x = lax.rem(me, 2)
        beside = me + 1 - 2 * x

        def qkv_copy(slab):
            return remote(
                qkv_send.at[slab],
                qkv_recv.at[slab],
                qkv_sems.at[0, slab],
                qkv_sems.at[1, slab],
                beside,
                core,
            )

        @pl.when(step == 0)
        def _():
            hello([(beside, core)])
            first_turned[...] = first_ref[...].T
            met([(beside, core)])
            start()

        lane = lax.broadcasted_iota(jnp.int32, (1, PAIR), 1)
        sides = [(lane < HEAD_DIM).astype(F32).astype(BF16), (lane >= HEAD_DIM).astype(F32).astype(BF16)]
        turned = k_ref[0].T
        ones = jnp.broadcast_to((lane < 2).astype(F32), (total, PAIR)).astype(BF16)
        values = jnp.concatenate([v_ref[0], ones], axis=1)

        def give(frame):
            keys = FRAME * (frame + 1)
            own = slice(frame * FRAME, keys)
            scaled = (g_ref[own, :].astype(F32) * r_ref[own, :]).astype(BF16)
            inner = scaled.astype(F32) * o_ref[own, :].astype(F32)
            grads, q_parts, g_parts = [], [], []
            for side in range(2):
                delta = jnp.sum(
                    jnp.where((lane < HEAD_DIM) == (side == 0), inner, 0.0), axis=1, keepdims=True
                )
                coarse = delta.astype(BF16).astype(F32)
                rest = jnp.where(lane == 0, -coarse, jnp.where(lane == 1, coarse - delta, 0.0))
                g2 = scaled * sides[side]
                grads.append(nt(values[:keys], jnp.concatenate([g2, rest.astype(BF16)], axis=1)))
                q_parts.append(q_ref[0, own, :] * sides[side])
                g_parts.append(g2)
            return grads, jnp.concatenate(q_parts, axis=0), jnp.concatenate(g_parts, axis=0)

        given = give(chunks - 1)
        for frame in reversed(range(chunks)):
            keys = FRAME * (frame + 1)
            own = slice(frame * FRAME, keys)
            tables = tables_of(fixed_ref, frames_ref, frame)
            grads, q_part, g_part = given
            given = give(frame - 1) if frame else None
            query_parts, score_parts, prob_parts = [], [], []
            for side in range(2):
                attention = p_ref[frame, side, :keys, :]
                grad_scores = (attention.astype(F32) * grads[side]).astype(BF16)
                query_parts.append(nn(turned[side * HEAD_DIM : (side + 1) * HEAD_DIM, :keys], grad_scores))
                score_parts.append(grad_scores)
                prob_parts.append(attention)
            grad_query = jnp.concatenate(query_parts, axis=0).T
            key_parts = nn(jnp.concatenate(score_parts, axis=1), q_part)
            value_parts = nn(jnp.concatenate(prob_parts, axis=1), g_part)
            dq_ref[own, :] = (turn(grad_query, tables, True) * SCORE_SCALE).astype(BF16)
            if frame == chunks - 1:
                dk_sum[...] = key_parts
                dv_sum[...] = value_parts
            else:
                dk_sum[:keys, :] += key_parts
                dv_sum[:keys, :] += value_parts
            dk_ref[own, :] = turn(dk_sum[own, :], tables, True).astype(BF16)
            dv_ref[own, :] = dv_sum[own, :].astype(BF16)

        for part, ref in enumerate((dq_ref, dk_ref, dv_ref)):
            piece = slice(part * PAIR, (part + 1) * PAIR)
            terms = nn(first_turned[...], ref[...])
            if swap_qkv:
                qkv_own[step, :, piece] = terms
                qkv_send[step, :, piece] = qkv_own[step, at((1 - x) * half, half), piece].astype(BF16)
            else:
                qkv_out[:, at(part * features + step * PAIR, PAIR)] = terms
        if swap_qkv:
            qkv_copy(step).start()

        @pl.when(step == slabs - 1)
        def _():
            finish()
            for slab in range(slabs if swap_qkv else 0):
                qkv_copy(slab).wait_recv()
                for part in range(3):
                    piece = slice(part * PAIR, (part + 1) * PAIR)
                    place = part * features + slab * PAIR
                    qkv_out[:, place : place + PAIR] = qkv_own[
                        slab, at(x * half, half), piece
                    ] + qkv_recv[slab, :, piece].astype(F32)
            for slab in range(slabs if swap_qkv else 0):
                qkv_copy(slab).wait_send()

    slab = pl.BlockSpec((total, PAIR), lambda s: (0, s))
    in_specs = [pl.BlockSpec((chunks, 2, total, FRAME), lambda s: (0, s, 0, 0))]
    in_specs += [slab] * 2
    for part in range(3):
        in_specs.append(pl.BlockSpec((1, total, PAIR), lambda s, part=part: (part, 0, s)))
    in_specs += [slab] + [whole(first), whole(fixed), whole(frames)]
    in_specs += swap.in_specs()
    qkv_shape = (half if swap_qkv else PAIR, 3 * features)
    shapes, specs = swap.outputs()
    out_shape = [jax.ShapeDtypeStruct((total, features), BF16)] * 3
    out_shape += [jax.ShapeDtypeStruct(qkv_shape, F32)] + shapes
    out_specs = [slab] * 3 + [whole_out(qkv_shape)] + specs
    scratch = [pltpu.VMEM((total, PAIR), F32)] * 2 + [pltpu.VMEM((PAIR, total), BF16)]
    if swap_qkv:
        scratch += [pltpu.VMEM((slabs, PAIR, 3 * PAIR), F32)]
        scratch += [pltpu.VMEM((slabs, half, 3 * PAIR), BF16)] * 2
        scratch += [pltpu.SemaphoreType.DMA((2, slabs))]
    scratch += swap.scratch()
    return pl.pallas_call(
        kernel,
        grid=(slabs,),
        out_shape=out_shape,
        in_specs=in_specs,
        out_specs=out_specs,
        scratch_shapes=scratch,
        compiler_params=pltpu.CompilerParams(
            collective_id=identity, has_side_effects=True, vmem_limit_bytes=VMEM_BYTES
        ),
        name=f"attention_backward_{identity}",
    )(
        probs,
        divisor,
        mixed,
        turned_qkv,
        turned_qkv,
        turned_qkv,
        grad_mixed,
        first,
        fixed,
        frames,
        *swap.operands(),
    )


def rows_backward(entry, upper, identity, span, swap):
    top, bottom = len(entry) == 1, upper is None
    if not top:
        above, entry = entry[0], entry[1:]
    total = entry[0].shape[1] if top else entry[0].shape[0]
    chunks = total // span
    columns = 256
    ahead = 0 if top else 2 if bottom else 1
    if top:
        width = 2 * entry[0].shape[2]
    else:
        features, width = entry[0].shape[1], entry[5].shape[1]
    if not bottom:
        layer = upper[0]
        hidden_units, mixed_features = upper[1].shape[1], upper[6].shape[1]
    place_rows = total // lax.axis_size("seq")

    def kernel(*refs):
        refs = list(refs)

        def take(count):
            taken = refs[:count]
            del refs[:count]
            return taken

        if top:
            (d_out_ref,) = take(1)
        else:
            dq_ref, dk_ref, dv_ref, unit1, scale1, dm_ref, wq, gain1 = take(8)
        if not bottom:
            act_ref, gp_ref, unit2, scale2, second_ref, mixed_ref = take(6)
            wo_any, wu_any, wd_any, gain2 = take(4)
        sources = take(swap.count)
        if not top:
            (vec1,) = take(1)
        if not bottom:
            dmid_out, dmix_out, out_sum, up_sum, down_sum, vec2 = take(6)
        else:
            dx_out, dx_other, vec_other = take(3)
        targets = take(swap.count)
        if not top:
            a_send, a_recv = take(2)
        if not bottom:
            b_send, b_recv, grad_keep, hidden_keep, low_keep, last_keep, wo, wu, wd, w_sem = take(10)
        else:
            dx_keep, dx_send, dx_recv, vec_recv, x_send_sem, x_recv_sem = take(6)
        send_sem, recv_sem = take(2)
        start_swap, finish_swap = swap.bind(sources, targets, refs)

        step = pl.program_id(0)
        me, core = lax.axis_index("seq"), lax.axis_index("tp")
        pair = at((me // 2) * PAIR, PAIR)
        x = lax.rem(me, 2)
        beside = me + 1 - 2 * x

        def exchange(kind, chunk):
            source, target = (a_send, a_recv) if kind == 0 else (b_send, b_recv)
            return remote(
                source.at[chunk],
                target.at[chunk],
                send_sem.at[kind, chunk],
                recv_sem.at[kind, chunk],
                me,
                1 - core,
            )

        def load(index):
            source, target = ((wd_any, wd), (wu_any, wu), (wo_any, wo))[index]
            return pltpu.make_async_copy(source.at[layer], target, w_sem.at[index])

        partners = [(me, 1 - core)] + ([(beside, core)] if bottom or swap.count else [])

        @pl.when(step == 0)
        def _():
            if not bottom:
                for index in range(3):
                    load(index).start()
                out_sum[...] = jnp.zeros_like(out_sum)
                up_sum[...] = jnp.zeros_like(up_sum)
                down_sum[...] = jnp.zeros_like(down_sum)
                vec2[...] = jnp.zeros_like(vec2)
            if not top:
                vec1[...] = jnp.zeros_like(vec1)
            hello(partners)

        def meet():
            @pl.when(step == 0)
            def _():
                met(partners)
                start_swap()

        def entry_products():
            partial = None
            for part, ref in enumerate((dq_ref, dk_ref, dv_ref)):
                grad = ref[...]
                term = nt(grad, wq[0, part])
                partial = term if partial is None else partial + term
                vec1[part : part + 1, :] += column_sum(grad.astype(F32))
            a_send[step] = partial.astype(BF16)

        def entry_norm(chunk):
            if top:
                return halves(d_out_ref)
            grad_first = a_send[chunk].astype(F32) + a_recv[chunk].astype(F32)
            unit, scale = kept_norm(unit1, scale1)
            for start, sums in ((3, column_sum(grad_first * unit)), (5, column_sum(grad_first))):
                for side in range(width // features):
                    piece = slice(side * features, (side + 1) * features)
                    vec1[start + side : start + side + 1, :] += sums[:, piece]
            return dm_ref[...] + norm_pull(grad_first, gain1[above : above + 1, :], unit, scale)

        def feed_forward(between=None):
            chunk = step - ahead
            gradient = entry_norm(chunk)
            if bottom:
                dx_keep[at(chunk * span, span), :] = gradient
                return
            grad_keep[lax.rem(chunk, 2)] = gradient
            vec2[1:2, :width] += column_sum(gradient)
            low = gradient.astype(BF16)
            low_keep[...] = low
            low_columns = low_keep[:, pair]
            second = second_ref[...]
            parts = [slice(start, start + columns) for start in range(0, hidden_units, columns)]
            grad_act = nt(low, wd[parts[0], :])
            for index, part in enumerate(parts):
                following = nt(low, wd[parts[index + 1], :]) if index + 1 < len(parts) else None
                grad_hidden = grad_act * gp_ref[:, part].astype(F32)
                hidden_keep[:, part] = grad_hidden.astype(BF16)
                vec2[0:1, part] += column_sum(grad_hidden)
                grad_act = following
            if between is not None:
                between()
            b_send[chunk] = nt(hidden_keep[...], wu[...]).astype(BF16)
            down_sum[...] += tn(low_columns, act_ref[...])
            up_sum[...] += tn(second, hidden_keep[...])

        def close():
            chunk = step - ahead - 1
            grad_second = b_send[chunk].astype(F32) + b_recv[chunk].astype(F32)
            unit, scale = kept_norm(unit2, scale2)
            vec2[2:3, :width] += column_sum(grad_second * unit)
            vec2[3:4, :width] += column_sum(grad_second)
            grad_middle = grad_keep[lax.rem(chunk, 2)] + norm_pull(
                grad_second, gain2[layer : layer + 1, :], unit, scale
            )
            dmid_out[...] = grad_middle
            vec2[4:5, :width] += column_sum(grad_middle)
            low = grad_middle.astype(BF16)
            last_keep[...] = low
            out_sum[...] += tn(last_keep[:, pair], mixed_ref[...])
            dmix_out[...] = nt(low, wo[...]).astype(BF16)

        if not top:

            @pl.when(step < chunks)
            def _():
                entry_products()
                meet()
                exchange(0, step).start()

        @pl.when((step >= ahead) & (step < chunks + ahead))
        def _():
            if not top:
                exchange(0, step - ahead).wait_recv()
            if not bottom:

                @pl.when(step == ahead)
                def _():
                    load(0).wait()

            feed_forward(lambda: pl.when(step == ahead)(lambda: load(1).wait()))
            if not bottom:
                if top:
                    meet()
                exchange(1, step - ahead).start()

        if not bottom:

            @pl.when(step == ahead + 1)
            def _():
                load(2).wait()

            @pl.when(step >= ahead + 1)
            def _():
                exchange(1, step - ahead - 1).wait_recv()
                close()

        if bottom:

            def x_copy(index):
                source, target = ((dx_send, dx_recv), (vec1, vec_recv))[index]
                return remote(
                    source, target, x_send_sem.at[index], x_recv_sem.at[index], beside, core
                )

            @pl.when(step == chunks + 1)
            def _():
                dx_send[...] = dx_keep[at(beside * place_rows, place_rows), :].astype(BF16)
                x_copy(0).start()
                x_copy(1).start()
                dx_out[...] = dx_keep[at(me * place_rows, place_rows), :]
                x_copy(0).wait_recv()
                x_copy(1).wait_recv()
                dx_other[...] = dx_recv[...].astype(F32)
                vec_other[...] = vec_recv[...]
                x_copy(0).wait_send()
                x_copy(1).wait_send()

        @pl.when(step == pl.num_programs(0) - 1)
        def _():
            for kind in ([] if top else [0]) + ([] if bottom else [1]):
                for chunk in range(chunks):
                    exchange(kind, chunk).wait_send()
            finish_swap()

    def rows(columns, behind):
        return pl.BlockSpec(
            (span, columns), lambda s: (jnp.clip(s - behind, 0, chunks - 1), 0)
        )

    vec = jax.ShapeDtypeStruct((8, VEC), F32)
    operands, in_specs, out_shape, out_specs, scratch = [], [], [], [], []
    if top:
        operands += list(entry)
        in_specs += [halves_spec(entry[0].shape, chunks, 0, span)]
    else:
        operands += list(entry)
        in_specs += [rows(features, 0)] * 3
        in_specs += [rows(width, ahead), rows(PAIR, ahead), rows(width, ahead)]
        in_specs += [
            pl.BlockSpec(
                (1, *entry[6].shape[1:]),
                lambda s: (above, 0, 0, 0),
                pipeline_mode=pl.Buffered(1),
            ),
            whole(entry[7]),
        ]
        narrow = jax.ShapeDtypeStruct((8, features), F32)
        out_shape += [narrow]
        out_specs += [whole_out((8, features))]
        scratch += [pltpu.VMEM((chunks, span, width), BF16)] * 2
    if not bottom:
        operands += list(upper[1:])
        in_specs += [rows(hidden_units, ahead)] * 2
        in_specs += [rows(width, ahead + 1), rows(PAIR, ahead + 1), rows(PAIR, ahead)]
        in_specs += [rows(mixed_features, ahead + 1)] + [ANYWHERE] * 3 + [whole(upper[10])]
        sums = [mixed_features, hidden_units, hidden_units]
        out_shape += [
            jax.ShapeDtypeStruct((total, width), F32),
            jax.ShapeDtypeStruct((total, mixed_features), BF16),
        ]
        out_shape += [jax.ShapeDtypeStruct((PAIR, size), F32) for size in sums] + [vec]
        out_specs += [rows(width, ahead + 1), rows(mixed_features, ahead + 1)]
        out_specs += [whole_out((PAIR, size)) for size in sums] + [whole_out((8, VEC))]
        scratch += [pltpu.VMEM((chunks, span, width), BF16)] * 2
        scratch += [
            pltpu.VMEM((2, span, width), F32),
            pltpu.VMEM((span, hidden_units), BF16),
            pltpu.VMEM((span, width), BF16),
            pltpu.VMEM((span, width), BF16),
            pltpu.VMEM(upper[7].shape[1:], BF16),
            pltpu.VMEM(upper[8].shape[1:], BF16),
            pltpu.VMEM(upper[9].shape[1:], BF16),
            pltpu.SemaphoreType.DMA((3,)),
        ]
    else:
        out_shape += [
            jax.ShapeDtypeStruct((place_rows, width), F32),
            jax.ShapeDtypeStruct((place_rows, width), F32),
            narrow,
        ]
        out_specs += [whole_out((place_rows, width))] * 2 + [whole_out((8, features))]
        scratch += [
            pltpu.VMEM((total, width), F32),
            pltpu.VMEM((place_rows, width), BF16),
            pltpu.VMEM((place_rows, width), BF16),
            pltpu.VMEM((8, features), F32),
            pltpu.SemaphoreType.DMA((2,)),
            pltpu.SemaphoreType.DMA((2,)),
        ]
    scratch += [pltpu.SemaphoreType.DMA((2, chunks))] * 2
    operands += swap.operands()
    in_specs += swap.in_specs()
    shapes, specs = swap.outputs()
    out_shape += shapes
    out_specs += specs
    scratch += swap.scratch()
    return pl.pallas_call(
        kernel,
        grid=(chunks + (1 if top else 2),),
        out_shape=out_shape,
        in_specs=in_specs,
        out_specs=out_specs,
        scratch_shapes=scratch,
        compiler_params=pltpu.CompilerParams(
            collective_id=identity, has_side_effects=True, vmem_limit_bytes=VMEM_BYTES
        ),
        name=f"rows_backward_{identity}",
    )(*operands)


def assemble(sums, vecs, lanes, n, features, hidden_units):
    place = lanes[1].shape[0]
    width = lanes[1].shape[1]
    half = PAIR // 2

    def kernel(*refs):
        refs = list(refs)

        def take(count):
            taken = refs[:count]
            del refs[:count]
            return taken

        qkvs, outs, ups, downs = take(LAYERS), take(LAYERS), take(LAYERS), take(LAYERS)
        vec_refs = [take(4) for _ in range(LAYERS)]
        out_lane, out_other, dx_own, dx_other = take(4)
        out_ref, dx_ref, gain1, shift1, g_qkv, b_qkv, g_out, b_out = take(8)
        gain2, shift2, g_up, b_up, g_down, b_down = take(6)
        out_own, sem = refs
        me = lax.axis_index("seq")
        x = lax.rem(me, 2)
        fetch = pltpu.make_async_copy(out_lane.at[at(me * place, place), :], out_own, sem)
        fetch.start()

        for layer in range(LAYERS):
            for part in range(3):
                g_qkv[layer, part] = qkvs[layer][:, part * features : (part + 1) * features]
            for ref, target in ((outs, g_out), (ups, g_up), (downs, g_down)):
                target[layer] = ref[layer][...]

        for layer, (entry_own, entry_other, upper_own, upper_other) in enumerate(vec_refs):
            line = slice(layer, layer + 1)
            for part in range(3):
                row = slice(part, part + 1)
                b_qkv[part, line, :] = entry_own[row, :] + entry_other[row, :]
            b_up[line, :] = upper_own[0:1, :hidden_units] + upper_other[0:1, :hidden_units]

            def owned(mine, other, row):
                wide = mine.shape[1]
                place = (me // 2) * PAIR
                pair = at(lax.rem(place, wide), PAIR)
                both = mine[row : row + 1, pair] + other[row : row + 1, pair]
                for later in range(1, width // wide):
                    line = slice(row + later, row + later + 1)
                    both = jnp.where(place // wide == later, mine[line, pair] + other[line, pair], both)
                return jnp.where(x == 0, both[:, :half], both[:, half:])

            gain1[line, :] = owned(entry_own, entry_other, 3)
            shift1[line, :] = owned(entry_own, entry_other, 5)
            b_down[line, :] = owned(upper_own, upper_other, 1)
            gain2[line, :] = owned(upper_own, upper_other, 2)
            shift2[line, :] = owned(upper_own, upper_other, 3)
            b_out[line, :] = owned(upper_own, upper_other, 4)

        def both_lanes(target, mine, other):
            target[:, 0, :] = jnp.where(x == 0, mine, other)
            target[:, 1, :] = jnp.where(x == 0, other, mine)

        both_lanes(dx_ref, dx_own[...], dx_other[...])
        fetch.wait()
        both_lanes(out_ref, out_own[...], out_other[...])

    def f32(*shape):
        return jax.ShapeDtypeStruct(shape, F32)

    in_vmem = pl.BlockSpec(memory_space=pltpu.VMEM)
    flat = []
    for kind in range(4):
        flat += [sums[layer][kind] for layer in range(LAYERS)]
    for layer in range(LAYERS):
        flat += list(vecs[layer])
    flat += list(lanes)
    small = f32(LAYERS, width // n)
    return pl.pallas_call(
        kernel,
        out_shape=(
            f32(place, 2, width),
            f32(place, 2, width),
            small,
            small,
            f32(LAYERS, 3, half, features),
            f32(3, LAYERS, features),
            f32(LAYERS, half, features),
            small,
            small,
            small,
            f32(LAYERS, half, hidden_units),
            f32(LAYERS, hidden_units),
            f32(LAYERS, half, hidden_units),
            small,
        ),
        in_specs=[in_vmem] * (len(flat) - 4) + [ANYWHERE] + [in_vmem] * 3,
        out_specs=(in_vmem,) * 14,
        scratch_shapes=[pltpu.VMEM((place, width), F32), pltpu.SemaphoreType.DMA],
        compiler_params=pltpu.CompilerParams(vmem_limit_bytes=VMEM_BYTES),
        name="assemble",
    )(*flat)


def per_chip(
    tokens,
    d_out,
    norm1_gain,
    norm1_shift,
    w_qkv,
    b_qkv,
    w_out,
    b_out,
    norm2_gain,
    norm2_shift,
    w_up,
    b_up,
    w_down,
    b_down,
    episode_frames,
    live,
):
    n = lax.axis_size("seq")
    rows = tokens.shape[0]
    features = w_qkv.shape[3]
    fixed, ahead = turn_constants(rows * n // FRAME)
    qkv, qkv_bias = w_qkv.transpose(0, 2, 1, 3), b_qkv.transpose(1, 0, 2)

    gathered, key_bias, frames, *projected = gather_and_project(
        tokens, live.T, episode_frames, norm1_gain, norm1_shift, qkv, qkv_bias, fixed, ahead, n
    )
    streams, kept, d_lane = [gathered], [], None
    for layer in range(LAYERS):
        following = None
        if layer + 1 < LAYERS:
            following = (qkv, norm1_gain, norm1_shift, qkv_bias, fixed, frames)
        results = layer_forward(
            layer,
            projected[0],
            key_bias,
            streams[layer],
            (w_out, w_up, w_down),
            (b_out, norm2_gain, norm2_shift, b_up, b_down),
            following,
            d_out if layer == 0 else None,
            n,
            1 + layer,
        )
        kept.append((*projected, *results[:8]))
        streams.append(results[8])
        if following is not None:
            projected = results[9:13]
        if layer == 0:
            d_lane = results[-1]

    sums = [[None] * 4 for _ in range(LAYERS)]
    vecs = [[None] * 4 for _ in range(LAYERS)]
    entry, later = (d_lane,), None
    for layer in reversed(range(LAYERS)):
        turned, first, unit1, scale1, probs, divisor, mixed = kept[layer][:7]
        unit2, scale2, second, act, slope = kept[layer][7:]
        upper = (
            layer,
            act,
            slope,
            unit2,
            scale2,
            second,
            mixed,
            w_out,
            w_up,
            w_down,
            norm2_gain,
        )
        identity = 1 + LAYERS + 2 * (LAYERS - 1 - layer)
        if later is None:
            results = rows_backward(entry, upper, identity, FRAME, Swap([], []))
        else:
            swap = Swap(later[:2], [(later[2], 0), (streams[LAYERS], rows)])
            vec1, *results = rows_backward(entry, upper, identity, FRAME, swap)
            results, swapped = results[:6], results[6:]
            sums[layer + 1][3], sums[layer + 1][0] = swapped[:2]
            vecs[layer + 1][3], out_other = swapped[2:]
            vecs[layer + 1][0] = vec1
        grad_middle, grad_mixed, out_sum, up_sum, down_sum, vec2 = results
        vecs[layer][2] = vec2
        last = layer == 0
        if last:
            swap = Swap([out_sum, up_sum], [(vec2, 0), (vecs[layer + 1][0], 0)])
        else:
            swap = Swap([out_sum, up_sum], [])
        results = attention_backward(
            probs,
            divisor,
            mixed,
            turned,
            grad_mixed,
            first,
            fixed,
            frames,
            swap,
            last,
            identity + 1,
        )
        grad_query, grad_key, grad_value, qkv_sum = results[:4]
        if last:
            sums[layer][:3] = [qkv_sum, *results[4:6]]
            vecs[layer][3], vecs[layer + 1][1] = results[6:8]
        else:
            sums[layer][1:3] = results[4:6]
            later = [down_sum, qkv_sum, vec2]
        entry = (
            layer,
            grad_query,
            grad_key,
            grad_value,
            unit1,
            scale1,
            grad_middle,
            qkv,
            norm1_gain,
        )
    vec1, dx_own, dx_other, vec_other, sums[0][3] = rows_backward(
        entry, None, 1 + 3 * LAYERS, FRAME, Swap([down_sum], [])
    )
    vecs[0][:2] = [vec1, vec_other]
    results = list(
        assemble(
            sums,
            vecs,
            (streams[LAYERS], out_other, dx_own, dx_other),
            n,
            features,
            w_up.shape[2],
        )
    )
    results[4] = results[4].transpose(0, 2, 1, 3)
    results[5] = results[5].transpose(1, 0, 2)
    results[6] = results[6].transpose(0, 2, 1)
    results[12] = results[12].transpose(0, 2, 1)
    return tuple(results)


def lane_fits(mesh, tokens):
    n = mesh.shape["seq"]
    positions, lanes, width = tokens.shape
    rows = positions // n
    return (
        lanes == 2
        and n % 4 == 0
        and positions <= 4 * FRAME
        and positions % FRAME == 0
        and FRAME % rows == 0
        and width // n * 2 == PAIR
        and mesh.shape["tp"] == 2
    )


def solution(mesh):
    placed = (
        P("seq", None, None),
        P("seq", None, None),
        P(),
        P(),
        P(None, None, None, "tp"),
        P(None, None, "tp"),
        P(None, "tp", None),
        P(),
        P(),
        P(),
        P(None, None, "tp"),
        P(None, "tp"),
        P(None, "tp", None),
        P(),
        P(),
        P("seq", None),
    )
    def mapped(body):
        return jax.shard_map(
            body,
            mesh=mesh,
            in_specs=placed,
            out_specs=(
                P("seq", None, None),
                P("seq", None, None),
                P(None, "seq"),
                P(None, "seq"),
                P(None, "seq", None, "tp"),
                P(None, None, "tp"),
                P(None, "tp", "seq"),
                P(None, "seq"),
                P(None, "seq"),
                P(None, "seq"),
                P(None, "seq", "tp"),
                P(None, "tp"),
                P(None, "tp", "seq"),
                P(None, "seq"),
            ),
            check_vma=False,
        )

    def run(tokens, *others):
        if lane_fits(mesh, tokens):
            return mapped(per_chip)(tokens, *others)
        return mapped(per_device)(tokens, *others)

    return run
```

profile of v0, /device:TPU:0, one launch (start us, length us, event | category | flops | bytes accessed | tf_op | source)
XLA Modules:
  0.0 246.0 jit_solution(12773628710776120071)
XLA Ops:
  0.6 35.6 %gather_and_project.1 = (bf16[2,1024,512]{2,1,0:T(8,128)(2,1)}, bf16[1024,128]{1,0:T(8,128)(2,1)}, f32[3,8,128]{2,1,0:T(8,128)}, bf16[3,1024,512]{2,1,0:T(8,128)...) custom-call(bf16[64,2,1024]{2,1,0:T(2,128)(2,1)} %refs_0_.1, s32[2,64]{1,0:T(2,128)} %bitcast.13, ...), custom_call_target="tpu_custom_call" | custom-call | tf_op jit(solution)/shard_map/gather_and_project/pallas_call | solution.py:881
  36.2 52.1 %layer_forward_0.1 = (bf16[4,8,1024,256]{3,2,1,0:T(8,128)(2,1)}, f32[1024,512]{1,0:T(8,128)}, bf16[1024,512]{1,0:T(8,128)(2,1)}, bf16[1024,1024]{1,0:T(8,128)(2,...) custom-call(bf16[3,1024,512]{2,1,0:T(8,128)(2,1)} %get-tuple-element, ...), custom_call_target="tpu_custom_call" | custom-call | tf_op jit(solution)/shard_map/layer_forward_0/pallas_call | solution.py:1217
  88.3 36.5 %layer_forward_1.1 = (bf16[4,8,1024,256]{3,2,1,0:T(8,128)(2,1)}, f32[1024,512]{1,0:T(8,128)}, bf16[1024,512]{1,0:T(8,128)(2,1)}, bf16[1024,1024]{1,0:T(8,128)(2,...) custom-call(bf16[3,1024,512]{2,1,0:T(8,128)(2,1)} %get-tuple-element, ...), custom_call_target="tpu_custom_call" | custom-call | tf_op jit(solution)/shard_map/layer_forward_1/pallas_call | solution.py:1217
  124.8 24.7 %rows_backward_3.1 = (f32[1024,1024]{1,0:T(8,128)}, bf16[1024,512]{1,0:T(8,128)(2,1)}, f32[128,512]{1,0:T(8,128)}, f32[128,2048]{1,0:T(8,128)}, f32[128,2048]{1,0:T(8,128)}, /*index=5*/f32[8,2048]{1,0:T(8,128)}) custom-call(bf16[2,1024,512]{2,1,0:T(8,128)(2,1)} %get-tuple-element.106.refs_0_, bf16[1024,2048]{1,0:T(8,128)(2,1)} %get-tuple-element.107.refs_1_, ...), custom_call_target="tpu_custom_call" | custom-call | tf_op jit(solution)/shard_map/rows_backward_3/pallas_call | solution.py:1750
  149.4 19.2 %attention_backward_4.1 = (bf16[1024,512]{1,0:T(8,128)(2,1)}, bf16[1024,512]{1,0:T(8,128)(2,1)}, bf16[1024,512]{1,0:T(8,128)(2,1)}, f32[128,1536]{1,0:T(8,128)}, f32[64,512]{1,0:T(8,128)}, /*index=5*/f32[64,2048]{1,0:T(8,128)}) custom-call(bf16[4,8,1024,256]{3,2,1,0:T(8,128)(2,1)} %get-tuple-element.103.refs_0_, f32[1024,512]{1,0:T(8,128)} %get-tuple-element.104.refs_1_, ...), custom_call_target="tpu_custom_call" | custom-call | tf_op jit(solution)/shard_map/attention_backward_4/pallas_call | solution.py:1436
  168.6 32.2 %rows_backward_5.1 = (f32[8,512]{1,0:T(8,128)}, f32[1024,1024]{1,0:T(8,128)}, bf16[1024,512]{1,0:T(8,128)(2,1)}, f32[128,512]{1,0:T(8,128)}, f32[128,2048]{1,0:T...) custom-call(bf16[1024,512]{1,0:T(8,128)(2,1)} %get-tuple-element.116, ...), custom_call_target="tpu_custom_call" | custom-call | tf_op jit(solution)/shard_map/rows_backward_5/pallas_call | solution.py:1750
  200.8 22.7 %attention_backward_6.1 = (bf16[1024,512]{1,0:T(8,128)(2,1)}, bf16[1024,512]{1,0:T(8,128)(2,1)}, bf16[1024,512]{1,0:T(8,128)(2,1)}, f32[64,1536]{1,0:T(8,128)}, ...) custom-call(bf16[4,8,1024,256]{3,2,1,0:T(8,128)(2,1)} %get-tuple-element.98.refs_0_, ...), custom_call_target="tpu_custom_call" | custom-call | tf_op jit(solution)/shard_map/attention_backward_6/pallas_call | solution.py:1436
  223.6 17.0 %rows_backward_7.1 = (f32[8,512]{1,0:T(8,128)}, f32[64,1024]{1,0:T(8,128)}, f32[64,1024]{1,0:T(8,128)}, f32[8,512]{1,0:T(8,128)}, f32[64,2048]{1,0:T(8,128)}) custom-call(bf16[1024,512]{1,0:T(8,128)(2,1)} %get-tuple-element.143.refs_0_, bf16[1024,512]{1,0:T(8,128)(2,1)} %get-tuple-element.144.refs_1_, bf16[1024,512]{1,0:T(8,128)(2,1)} %get-tuple-element.145.refs_2_, ...), custom_call_target="tpu_custom_call" | custom-call | tf_op jit(solution)/shard_map/rows_backward_7/pallas_call | solution.py:1750
  240.5 5.3 %assemble.1 = (f32[64,2,1024]{2,1,0:T(2,128)}, f32[64,2,1024]{2,1,0:T(2,128)}, f32[2,64]{1,0:T(2,128)}, f32[2,64]{1,0:T(2,128)}, f32[2,3,64,512]{3,2,1,0:T(8,128...) custom-call(f32[64,1536]{1,0:T(8,128)} %get-tuple-element.137.refs_0, ...), custom_call_target="tpu_custom_call" | custom-call | tf_op jit(solution)/shard_map/assemble/pallas_call | solution.py:1837
where the time goes:
time: 251 us; the launch traced here: 246 us
  Pallas kernels  245 us (98%)
    pallas_call x2, Pallas kernels, layer_forward(): pl.pallas_call(kernel, grid=(chunks + 2,), out_shape=out_shape, in_specs=...  88.5 us
    pallas_call x3, Pallas kernels, rows_backward(): pl.pallas_call(kernel, grid=(chunks + (1 if top else 2),), out_shape=out_...  73.9 us
    pallas_call x2, Pallas kernels, attention_backward(): pl.pallas_call(kernel, grid=(slabs,), out_shape=out_shape, in_specs=in_sp...  41.9 us
    pallas_call x1, Pallas kernels, gather_and_project(): pl.pallas_call(kernel, out_shape=(jax.ShapeDtypeStruct((2, total, half),...  35.6 us
    pallas_call x1, Pallas kernels, assemble(): pl.pallas_call(kernel, out_shape=(f32(place, 2, width), f32(place, 2, wid...  5.29 us

commit v1 on v0

--- a/solution.py
+++ b/solution.py
@@ -851,13 +851,11 @@
 
         for event in range(relay.events):
             relay.arrive(event)
+        for event in range(relay.events):
+            relay.complete(event)
             if event:
-                relay.complete(event - 1)
-            if event > 1:
-                project_frame(relay.ready(event - 2))
-        relay.complete(relay.events - 1)
-        for event in range(max(0, relay.events - 2), relay.events):
-            project_frame(relay.ready(event))
+                project_frame(relay.ready(event - 1))
+        project_frame(relay.ready(relay.events - 1))
         relay.finish()
 
         for key_frame in range(chunks):
@@ -1047,24 +1045,6 @@
             a_send[step] = nn(mixed_ref[...], wo[...]).astype(BF16)
             exchange(0, step).start()
 
-        if relay is not None:
-            for event in range(relay.events):
-
-                @pl.when(step == 2 + event // 2)
-                def _():
-                    relay.arrive(event)
-
-                @pl.when(step == 3 + event // 2)
-                def _():
-                    relay.complete(event)
-
-            @pl.when(step == chunks + 1)
-            def _():
-                for event in range(relay.events):
-                    relay.ready(event)
-                relay.finish()
-                pltpu.make_async_copy(buffer, d_all, d_sem).start()
-
         def feed_forward():
             chunk = step - 1
             middle = (halves(x_ref) if split else x_ref[...]) + (
@@ -1124,6 +1104,24 @@
         def _():
             exchange(1, step - 2).wait_recv()
             close()
+
+        if relay is not None:
+            for event in range(relay.events):
+
+                @pl.when(step == 1 + event // 2)
+                def _():
+                    relay.arrive(event)
+
+                @pl.when(step == 2 + event // 2)
+                def _():
+                    relay.complete(event)
+
+            @pl.when(step == chunks + 1)
+            def _():
+                for event in range(relay.events):
+                    relay.ready(event)
+                relay.finish()
+                pltpu.make_async_copy(buffer, d_all, d_sem).start()
 
         @pl.when(step == chunks + 1)
         def _():
@@ -1583,13 +1581,30 @@
             low_columns = low_keep[:, pair]
             second = second_ref[...]
             parts = [slice(start, start + columns) for start in range(0, hidden_units, columns)]
-            grad_act = nt(low, wd[parts[0], :])
-            for index, part in enumerate(parts):
-                following = nt(low, wd[parts[index + 1], :]) if index + 1 < len(parts) else None
-                grad_hidden = grad_act * gp_ref[:, part].astype(F32)
-                hidden_keep[:, part] = grad_hidden.astype(BF16)
-                vec2[0:1, part] += column_sum(grad_hidden)
-                grad_act = following
+            if not top:
+                wide = 4 * columns
+
+                def some(index):
+                    start = index * wide
+                    places = [pl.ds(pl.multiple_of(start + k * columns, columns), columns) for k in range(4)]
+                    grad_act = nt(low_keep[...], wd[places[0], :])
+                    for k, part in enumerate(places):
+                        following = nt(low_keep[...], wd[places[k + 1], :]) if k < 3 else None
+                        grad_hidden = grad_act * gp_ref[:, part].astype(F32)
+                        hidden_keep[:, part] = grad_hidden.astype(BF16)
+                        vec2[0:1, part] += column_sum(grad_hidden)
+                        grad_act = following
+
+                repeat(hidden_units // wide, some)
+            else:
+                grad_act = nt(low, wd[parts[0], :])
+                for index, part in enumerate(parts):
+                    following = nt(low, wd[parts[index + 1], :]) if index + 1 < len(parts) else None
+                    grad_hidden = grad_act * gp_ref[:, part].astype(F32)
+                    hidden_keep[:, part] = grad_hidden.astype(BF16)
+                    vec2[0:1, part] += column_sum(grad_hidden)
+                    grad_act = following
+
             if between is not None:
                 between()
             b_send[chunk] = nt(hidden_keep[...], wu[...]).astype(BF16)
@@ -1779,7 +1794,7 @@
         out_lane, out_other, dx_own, dx_other = take(4)
         out_ref, dx_ref, gain1, shift1, g_qkv, b_qkv, g_out, b_out = take(8)
         gain2, shift2, g_up, b_up, g_down, b_down = take(6)
-        out_own, sem = refs
+        out_own, sem, lane_sems = refs
         me = lax.axis_index("seq")
         x = lax.rem(me, 2)
         fetch = pltpu.make_async_copy(out_lane.at[at(me * place, place), :], out_own, sem)
@@ -1815,13 +1830,29 @@
             shift2[line, :] = owned(upper_own, upper_other, 3)
             b_out[line, :] = owned(upper_own, upper_other, 4)
 
-        def both_lanes(target, mine, other):
-            target[:, 0, :] = jnp.where(x == 0, mine, other)
-            target[:, 1, :] = jnp.where(x == 0, other, mine)
-
-        both_lanes(dx_ref, dx_own[...], dx_other[...])
         fetch.wait()
-        both_lanes(out_ref, out_own[...], out_other[...])
+
+        def lane_copies(lane):
+            return [
+                pltpu.make_async_copy(source, target.at[:, place_of, :], lane_sems.at[index])
+                for index, (source, target, place_of) in enumerate(
+                    (
+                        (out_own, out_ref, lane),
+                        (out_other, out_ref, 1 - lane),
+                        (dx_own, dx_ref, lane),
+                        (dx_other, dx_ref, 1 - lane),
+                    )
+                )
+            ]
+
+        for lane in range(2):
+
+            @pl.when(x == lane)
+            def _():
+                for copy in lane_copies(lane):
+                    copy.start()
+                for copy in lane_copies(lane):
+                    copy.wait()
 
     def f32(*shape):
         return jax.ShapeDtypeStruct(shape, F32)
@@ -1853,8 +1884,12 @@
             small,
         ),
         in_specs=[in_vmem] * (len(flat) - 4) + [ANYWHERE] + [in_vmem] * 3,
-        out_specs=(in_vmem,) * 14,
-        scratch_shapes=[pltpu.VMEM((place, width), F32), pltpu.SemaphoreType.DMA],
+        out_specs=(ANYWHERE,) * 2 + (in_vmem,) * 12,
+        scratch_shapes=[
+            pltpu.VMEM((place, width), F32),
+            pltpu.SemaphoreType.DMA,
+            pltpu.SemaphoreType.DMA((4,)),
+        ],
         compiler_params=pltpu.CompilerParams(vmem_limit_bytes=VMEM_BYTES),
         name="assemble",
     )(*flat)

time: 251 us -> 254 us (1.012)
  Pallas kernels: 245 us -> 249 us
where the time goes in v1:
time: 254 us; the launch traced here: 250 us
  Pallas kernels  249 us (98%)
    pallas_call x2, Pallas kernels, layer_forward(): pl.pallas_call(kernel, grid=(chunks + 2,), out_shape=out_shape, in_specs=...  89.5 us
    pallas_call x3, Pallas kernels, rows_backward(): pl.pallas_call(kernel, grid=(chunks + (1 if top else 2),), out_shape=out_...  75.6 us
    pallas_call x2, Pallas kernels, attention_backward(): pl.pallas_call(kernel, grid=(slabs,), out_shape=out_shape, in_specs=in_sp...  41.9 us
    pallas_call x1, Pallas kernels, gather_and_project(): pl.pallas_call(kernel, out_shape=(jax.ShapeDtypeStruct((2, total, half),...  36 us
    pallas_call x1, Pallas kernels, assemble(): pl.pallas_call(kernel, out_shape=(f32(place, 2, width), f32(place, 2, wid...  5.93 us

profile of v1, /device:TPU:0, one launch (start us, length us, event | category | flops | bytes accessed | tf_op | source)
XLA Modules:
  0.0 249.8 jit_solution(10055158937967226337)
XLA Ops:
  0.6 36.0 %gather_and_project.1 = (bf16[2,1024,512]{2,1,0:T(8,128)(2,1)}, bf16[1024,128]{1,0:T(8,128)(2,1)}, f32[3,8,128]{2,1,0:T(8,128)}, bf16[3,1024,512]{2,1,0:T(8,128)...) custom-call(bf16[64,2,1024]{2,1,0:T(2,128)(2,1)} %refs_0_.1, s32[2,64]{1,0:T(2,128)} %bitcast.13, ...), custom_call_target="tpu_custom_call" | custom-call | tf_op jit(solution)/shard_map/gather_and_project/pallas_call | solution.py:879
  36.6 53.0 %layer_forward_0.1 = (bf16[4,8,1024,256]{3,2,1,0:T(8,128)(2,1)}, f32[1024,512]{1,0:T(8,128)}, bf16[1024,512]{1,0:T(8,128)(2,1)}, bf16[1024,1024]{1,0:T(8,128)(2,...) custom-call(bf16[3,1024,512]{2,1,0:T(8,128)(2,1)} %get-tuple-element, ...), custom_call_target="tpu_custom_call" | custom-call | tf_op jit(solution)/shard_map/layer_forward_0/pallas_call | solution.py:1215
  89.7 36.5 %layer_forward_1.1 = (bf16[4,8,1024,256]{3,2,1,0:T(8,128)(2,1)}, f32[1024,512]{1,0:T(8,128)}, bf16[1024,512]{1,0:T(8,128)(2,1)}, bf16[1024,1024]{1,0:T(8,128)(2,...) custom-call(bf16[3,1024,512]{2,1,0:T(8,128)(2,1)} %get-tuple-element, ...), custom_call_target="tpu_custom_call" | custom-call | tf_op jit(solution)/shard_map/layer_forward_1/pallas_call | solution.py:1215
  126.2 24.7 %rows_backward_3.1 = (f32[1024,1024]{1,0:T(8,128)}, bf16[1024,512]{1,0:T(8,128)(2,1)}, f32[128,512]{1,0:T(8,128)}, f32[128,2048]{1,0:T(8,128)}, f32[128,2048]{1,0:T(8,128)}, /*index=5*/f32[8,2048]{1,0:T(8,128)}) custom-call(bf16[2,1024,512]{2,1,0:T(8,128)(2,1)} %get-tuple-element.106.refs_0_, bf16[1024,2048]{1,0:T(8,128)(2,1)} %get-tuple-element.107.refs_1_, ...), custom_call_target="tpu_custom_call" | custom-call | tf_op jit(solution)/shard_map/rows_backward_3/pallas_call | solution.py:1765
  150.8 19.2 %attention_backward_4.1 = (bf16[1024,512]{1,0:T(8,128)(2,1)}, bf16[1024,512]{1,0:T(8,128)(2,1)}, bf16[1024,512]{1,0:T(8,128)(2,1)}, f32[128,1536]{1,0:T(8,128)}, f32[64,512]{1,0:T(8,128)}, /*index=5*/f32[64,2048]{1,0:T(8,128)}) custom-call(bf16[4,8,1024,256]{3,2,1,0:T(8,128)(2,1)} %get-tuple-element.103.refs_0_, f32[1024,512]{1,0:T(8,128)} %get-tuple-element.104.refs_1_, ...), custom_call_target="tpu_custom_call" | custom-call | tf_op jit(solution)/shard_map/attention_backward_4/pallas_call | solution.py:1434
  170.0 33.9 %rows_backward_5.1 = (f32[8,512]{1,0:T(8,128)}, f32[1024,1024]{1,0:T(8,128)}, bf16[1024,512]{1,0:T(8,128)(2,1)}, f32[128,512]{1,0:T(8,128)}, f32[128,2048]{1,0:T...) custom-call(bf16[1024,512]{1,0:T(8,128)(2,1)} %get-tuple-element.116, ...), custom_call_target="tpu_custom_call" | custom-call | tf_op jit(solution)/shard_map/rows_backward_5/pallas_call | solution.py:1765
  204.0 22.7 %attention_backward_6.1 = (bf16[1024,512]{1,0:T(8,128)(2,1)}, bf16[1024,512]{1,0:T(8,128)(2,1)}, bf16[1024,512]{1,0:T(8,128)(2,1)}, f32[64,1536]{1,0:T(8,128)}, ...) custom-call(bf16[4,8,1024,256]{3,2,1,0:T(8,128)(2,1)} %get-tuple-element.98.refs_0_, ...), custom_call_target="tpu_custom_call" | custom-call | tf_op jit(solution)/shard_map/attention_backward_6/pallas_call | solution.py:1434
  226.6 17.0 %rows_backward_7.1 = (f32[8,512]{1,0:T(8,128)}, f32[64,1024]{1,0:T(8,128)}, f32[64,1024]{1,0:T(8,128)}, f32[8,512]{1,0:T(8,128)}, f32[64,2048]{1,0:T(8,128)}) custom-call(bf16[1024,512]{1,0:T(8,128)(2,1)} %get-tuple-element.143.refs_0_, bf16[1024,512]{1,0:T(8,128)(2,1)} %get-tuple-element.144.refs_1_, bf16[1024,512]{1,0:T(8,128)(2,1)} %get-tuple-element.145.refs_2_, ...), custom_call_target="tpu_custom_call" | custom-call | tf_op jit(solution)/shard_map/rows_backward_7/pallas_call | solution.py:1765
  243.6 5.9 %assemble.1 = (f32[64,2,1024]{2,1,0:T(2,128)}, f32[64,2,1024]{2,1,0:T(2,128)}, f32[2,64]{1,0:T(2,128)}, f32[2,64]{1,0:T(2,128)}, f32[2,3,64,512]{3,2,1,0:T(8,128...) custom-call(f32[64,1536]{1,0:T(8,128)} %get-tuple-element.137.refs_0, ...), custom_call_target="tpu_custom_call" | custom-call | tf_op jit(solution)/shard_map/assemble/pallas_call | solution.py:1868
